TPU v7x, 256 devices: a whole 4x4x8 slice. The times are simulated.
256 devices in a mesh: section: 16 (over z_lo, y, core), expert: 16 (over z_hi, x).
Axes of the slice: x: 4, y: 4, z: 8 (z_hi: 4, z_lo: 2; z = z_hi * 2 + z_lo), core: 2. Of those that a mesh axis runs over, the one named last changes fastest.
Arguments:
- tokens: bfloat16 [32768, 4096], P(('section', 'expert')), may hold values from -6 to 6
- norm_gain: float32 [16, 4096], P('section'), may hold values from 0.1 to 1.9
- w_gate: bfloat16 [16, 4096, 6144], P('section', None, 'expert'), may hold values from -0.09375 to 0.09375
- w_up: bfloat16 [16, 4096, 6144], P('section', None, 'expert'), may hold values from -0.09375 to 0.09375
- w_down: bfloat16 [16, 6144, 4096], P('section', 'expert'), may hold values from -0.21875 to 0.21875
- route_ids: int32 [2, 32768, 2], P(None, ('section', 'expert')), may hold values from 0 to 7, all different within a row; in each aligned block of 128 rows (0 to 127, 128 to 255, ..., all dimensions but the last counted through in order) at most 40 rows name the same one
- route_weights: bfloat16 [2, 32768, 2], P(None, ('section', 'expert')), may hold values from 0.25 to 1
Outputs:
- mixture: bfloat16 [32768, 4096], P(('section', 'expert'))
Inputs may be any that keep to these rules, and one draw needn't show every extreme that they name: `route_ids`: in each aligned block of 128 rows of a loop step (the rows of one device), a row names 2 different experts, no expert is named by more than 40 rows, a bound that some block reaches.
All inputs are finite; a program needn't handle non-finite values.
Results may differ from a plain program's by a relative error of at most 0.0072.
Values may be sent and summed in bfloat16 or wider, within the bound.
No kernel may reach another device: no remote copies, remote signals or barrier semaphores. Data moves between devices by JAX's collectives and lax.ppermute only.
A program may use at most 64 MiB of HBM per device.

v0:
```python
import jax
import jax.numpy as jnp
from jax import lax
from jax.sharding import PartitionSpec as P


def shifted(block, axis, distance):
    devices = range(lax.axis_size(axis))
    route = [((i - distance) % len(devices), i) for i in devices]
    return lax.ppermute(block, axis, route)


def rms_norm(values, gain):
    wide = values.astype(jnp.float32)
    meansq = jnp.mean(wide * wide, axis=-1, keepdims=True)
    return (wide * lax.rsqrt(meansq + 1e-06) * gain).astype(jnp.bfloat16)


def slot_tables(ids, weights, experts, capacity):
    flat_ids = ids.reshape(-1)
    expert_range = jnp.arange(experts, dtype=jnp.int32)
    hot = (flat_ids[:, None] == expert_range[None, :]).astype(jnp.int32)
    ranks = jnp.cumsum(hot, axis=0) - 1
    slots = jnp.sum(hot * ranks, axis=1).reshape(ids.shape)
    hit_expert = (ids[:, :, None] == expert_range[None, None, :]).astype(jnp.float32)
    slot_range = jnp.arange(capacity, dtype=jnp.int32)
    hit_slot = (slots[:, :, None] == slot_range[None, None, :]).astype(jnp.float32)
    select = jnp.einsum("rke,rkc->ecr", hit_expert, hit_slot)
    combine = jnp.einsum("rke,rkc,rk->rec", hit_expert, hit_slot, weights.astype(jnp.float32))
    return (select, combine)


def section_layer(state, gain, gate_w, up_w, down_w, ids, weights):
    row_count, width = state.shape
    top_count = ids.shape[1]
    experts = lax.axis_size("expert") // 2
    capacity = row_count * top_count // experts + row_count // 16
    normed = rms_norm(state, gain)
    select, combine = slot_tables(ids, weights, experts, capacity)
    picked = jnp.einsum(
        "ecr,rd->ecd", select.astype(jnp.bfloat16), normed, preferred_element_type=jnp.float32
    ).astype(jnp.bfloat16)
    combine_bf = combine.astype(jnp.bfloat16)
    outgoing = jnp.repeat(picked, 2, axis=0)
    slot_rows = lax.all_to_all(outgoing, "expert", split_axis=0, concat_axis=0, tiled=True)
    gate_proj = jnp.einsum("ncd,df->ncf", slot_rows, gate_w, preferred_element_type=jnp.float32)
    up_proj = jnp.einsum("ncd,df->ncf", slot_rows, up_w, preferred_element_type=jnp.float32)
    hidden = (jax.nn.silu(gate_proj) * up_proj).astype(jnp.bfloat16)
    returned = lax.all_to_all(
        jnp.einsum("ncf,fd->ncd", hidden, down_w, preferred_element_type=jnp.float32).astype(
            jnp.bfloat16
        ),
        "expert",
        split_axis=0,
        concat_axis=0,
        tiled=True,
    )
    returned = returned.reshape(experts, 2, capacity, width)
    merged = (returned[:, 0].astype(jnp.float32) + returned[:, 1].astype(jnp.float32)).astype(
        jnp.bfloat16
    )
    mixed = jnp.einsum("rec,ecd->rd", combine_bf, merged, preferred_element_type=jnp.float32)
    return (state.astype(jnp.float32) + mixed).astype(jnp.bfloat16)


def per_device(tokens, norm_gain, w_gate, w_up, w_down, route_ids, route_weights):
    state = tokens
    for loop_step in range(route_ids.shape[0]):
        state = section_layer(
            state,
            norm_gain[0],
            w_gate[0],
            w_up[0],
            w_down[0],
            route_ids[loop_step],
            route_weights[loop_step],
        )
        state = shifted(state, "section", 1)
    return state


def solution(mesh):
    in_specs = (
        P(("section", "expert"), None),
        P("section", None),
        P("section", None, "expert"),
        P("section", None, "expert"),
        P("section", "expert", None),
        P(None, ("section", "expert"), None),
        P(None, ("section", "expert"), None),
    )
    out_specs = P(("section", "expert"), None)
    return jax.shard_map(
        per_device, mesh=mesh, in_specs=in_specs, out_specs=out_specs, check_vma=False
    )
```

profile of v0, /device:TPU:32, one launch (start us, length us, event | category | flops | bytes accessed | tf_op | source)
XLA Modules:
  0.0 575.4 jit_solution(15760956827419908573)
XLA Ops:
  1.3 1.5 fusion.18
  4.6 1.6 fusion.55
  6.5 2.1 convolution_convert_fusion.3
  9.3 129.9 %all_to_all.20 = bf16[16,40,4096]{2,1,0:T(8,128)(2,1)S(1)} all-to-all(bf16[16,40,4096]{2,1,0:T(8,128)(2,1)S(1)} %bitcast.113), channel_id=1, replica_groups=mesh['section'=16,'expert'=16] {'expert'}, dimensions={0} | all-to-all | bytes 10485760 | tf_op jit(solution)/shard_map/all_to_all | solution.py:45
  139.2 2.3 copy-done.1
  141.5 3.9 fusion.12
  145.4 11.6 %convolution_convert_fusion.1 = bf16[16,40,4096]{2,1,0:T(8,128)(2,1)} fusion(bf16[1,384,4096]{2,1,0:T(8,128)(2,1)S(1)} %copy-done, bf16[16,40,4096]{2,1,0:T(8,128)(2,1)} %copy-done.1, bf16[1,4096,384]{2,1,0:T(8,128)(2,1)} %param.10, f32[16,40,384]{2,1,0:T(8,128)} %fusion.12), kind=kOutput, calls=%fused_computation.1 | convolution fusion | flops 4030627840 | bytes 17760256 | tf_op jit(solution)/shard_map/ncf,fd->ncd/dot_general | solution.py:50
  157.0 4.7 all-to-all-start.1
  161.9 1.8 fusion.53
  163.9 119.2 %all-to-all-done.1 = bf16[16,40,4096]{2,1,0:T(8,128)(2,1)} async-done(((bf16[16,40,4096]{2,1,0:T(8,128)(2,1)}), bf16[16,40,4096]{2,1,0:T(8,128)(2,1)}, u32[]{:S(2)}, u32[]{:S(2)}) %all-to-all-start.1) | async-done | bytes 5242912 | tf_op jit(solution)/shard_map/all_to_all | solution.py:49
  283.1 4.8 fusion.3
  290.1 1.6 fusion.52
  292.0 12.6 %collective-permute-done = bf16[128,4096]{1,0:T(8,128)(2,1)} collective-permute-done((bf16[128,4096]{1,0:T(8,128)(2,1)}, bf16[128,4096]{1,0:T(8,128)(2,1)}, u32[]{:S(2)}, u32[]{:S(2)}) %collective-permute-start) | collective-permute-done | bytes 1048608 | tf_op jit(solution)/shard_map/ppermute | solution.py:10
  304.5 1.5 fusion.21
  306.1 2.2 convolution_convert_fusion.2
  308.9 120.6 %all_to_all.21 = bf16[16,40,4096]{2,1,0:T(8,128)(2,1)S(1)} all-to-all(bf16[16,40,4096]{2,1,0:T(8,128)(2,1)S(1)} %bitcast.114), channel_id=1, replica_groups=mesh['section'=16,'expert'=16] {'expert'}, dimensions={0} | all-to-all | bytes 10485760 | tf_op jit(solution)/shard_map/all_to_all | solution.py:45
  429.5 2.3 copy-done.2
  431.8 3.9 fusion.10
  435.7 11.6 %convolution_convert_fusion = bf16[16,40,4096]{2,1,0:T(8,128)(2,1)} fusion(bf16[1,384,4096]{2,1,0:T(8,128)(2,1)S(1)} %copy-done, bf16[16,40,4096]{2,1,0:T(8,128)(2,1)} %copy-done.2, bf16[1,4096,384]{2,1,0:T(8,128)(2,1)} %param.10, f32[16,40,384]{2,1,0:T(8,128)} %fusion.10), kind=kOutput, calls=%fused_computation | convolution fusion | flops 4030627840 | bytes 17760256 | tf_op jit(solution)/shard_map/ncf,fd->ncd/dot_general | solution.py:50
  447.3 19.1 %all-to-all-start.3 = ((bf16[16,40,4096]{2,1,0:T(8,128)(2,1)}), bf16[16,40,4096]{2,1,0:T(8,128)(2,1)}, u32[]{:S(2)}, u32[]{:S(2)}) async-start(bf16[16,40,4096]{2,1,0:T(8,128)(2,1)} %convolution_convert_fusion), calls=%async_computation.3 | async-start | bytes 10485760 | tf_op jit(solution)/shard_map/all_to_all | solution.py:49
  467.2 1.8 fusion.50
  469.1 85.0 %all-to-all-done.3 = bf16[16,40,4096]{2,1,0:T(8,128)(2,1)} async-done(((bf16[16,40,4096]{2,1,0:T(8,128)(2,1)}), bf16[16,40,4096]{2,1,0:T(8,128)(2,1)}, u32[]{:S(2)}, u32[]{:S(2)}) %all-to-all-start.3) | async-done | bytes 5242912 | tf_op jit(solution)/shard_map/all_to_all | solution.py:49
  554.1 3.9 fusion.2
  558.1 16.3 %collective-permute-done.1 = bf16[128,4096]{1,0:T(8,128)(2,1)S(1)} collective-permute-done((bf16[128,4096]{1,0:T(8,128)(2,1)S(1)}, bf16[128,4096]{1,0:T(8,128)(2,1)S(1)}, u32[]{:S(2)}, u32[]{:S(2)}) %collective-permute-start.1) | collective-permute-done | bytes 1048608 | tf_op jit(solution)/shard_map/ppermute | solution.py:10
  (59 shorter events, 9.3 us)
Async XLA Ops:
  0.0 145.4 %copy-start = (bf16[1,384,4096]{2,1,0:T(8,128)(2,1)S(1)}, bf16[1,384,4096]{2,1,0:T(8,128)(2,1)}, u32[]{:S(2)}) copy-start(bf16[1,384,4096]{2,1,0:T(8,128)(2,1)} %param.11) | copy-start | bytes 9437188
  0.0 6.5 %copy-start.3 = (f32[1,4096]{1,0:T(1,128)S(1)}, f32[1,4096]{1,0:T(1,128)}, u32[]{:S(2)}) copy-start(f32[1,4096]{1,0:T(1,128)} %param.8) | copy-start | bytes 49156
  2.9 1.7 copy-start.6
  9.3 132.2 %copy-start.10 = (bf16[1,4096,384]{2,1,0:T(8,128)(2,1)S(1)}, bf16[1,4096,384]{2,1,0:T(8,128)(2,1)}, u32[]{:S(2)}) copy-start(bf16[1,4096,384]{2,1,0:T(8,128)(2,1)} %param.9) | copy-start | bytes 9437188
  139.2 2.3 copy-start.1
  157.0 4.7 copy-start.9
  157.0 4.9 copy-start.7
  157.0 126.0 %all-to-all-start.1 = ((bf16[16,40,4096]{2,1,0:T(8,128)(2,1)}), bf16[16,40,4096]{2,1,0:T(8,128)(2,1)}, u32[]{:S(2)}, u32[]{:S(2)}) async-start(bf16[16,40,4096]{2,1,0:T(8,128)(2,1)} %convolution_convert_fusion.1), calls=%async_computation.1 | async-start | bytes 10485760 | tf_op jit(solution)/shard_map/all_to_all | solution.py:49
  287.9 16.6 %collective-permute-start = (bf16[128,4096]{1,0:T(8,128)(2,1)}, bf16[128,4096]{1,0:T(8,128)(2,1)}, u32[]{:S(2)}, u32[]{:S(2)}) collective-permute-start(bf16[128,4096]{1,0:T(8,128)(2,1)} %fusion.3), channel_id=1, source_target_pairs={{240,0},{0,16},{16,32},{32,48},{48,64},{64,80},{80,96},{96,112},{1... | collective-permute-start | bytes 3145736 | tf_op jit(solution)/shard_map/ppermute | solution.py:10
  288.4 1.7 copy-start.4
  308.9 122.9 %copy-start.11 = (bf16[1,4096,384]{2,1,0:T(8,128)(2,1)S(1)}, bf16[1,4096,384]{2,1,0:T(8,128)(2,1)}, u32[]{:S(2)}) copy-start(bf16[1,4096,384]{2,1,0:T(8,128)(2,1)} %param.9) | copy-start | bytes 9437188
  429.5 2.3 copy-start.2
  447.3 19.8 %copy-start.5 = (s32[128,2]{1,0:T(8,128)S(1)}, s32[128,2]{1,0:T(8,128)}, u32[]{:S(2)}) copy-start(s32[128,2]{1,0:T(8,128)} %copy-done.4) | copy-start | bytes 3076
  447.3 19.8 %copy-start.8 = (s32[128,2]{1,0:T(8,128)S(1)}, s32[128,2]{1,0:T(8,128)}, u32[]{:S(2)}) copy-start(s32[128,2]{1,0:T(8,128)} %eq.138) | copy-start | bytes 3076
  447.3 106.8 %all-to-all-start.3 = ((bf16[16,40,4096]{2,1,0:T(8,128)(2,1)}), bf16[16,40,4096]{2,1,0:T(8,128)(2,1)}, u32[]{:S(2)}, u32[]{:S(2)}) async-start(bf16[16,40,4096]{2,1,0:T(8,128)(2,1)} %convolution_convert_fusion), calls=%async_computation.3 | async-start | bytes 10485760 | tf_op jit(solution)/shard_map/all_to_all | solution.py:49
  558.0 16.4 %collective-permute-start.1 = (bf16[128,4096]{1,0:T(8,128)(2,1)S(1)}, bf16[128,4096]{1,0:T(8,128)(2,1)S(1)}, u32[]{:S(2)}, u32[]{:S(2)}) collective-permute-start(bf16[128,4096]{1,0:T(8,128)(2,1)S(1)} %fusion.2), channel_id=1, source_target_pairs={{240,0},{0,16},{16,32},{32,48},{48,64},{64,80},{80,96},{96,112},{1... | collective-permute-start | bytes 3145736 | tf_op jit(solution)/shard_map/ppermute | solution.py:10
where the time goes:
time: 583 us; the launch traced here: 575 us
  blocking collectives  250 us (43%)
  waiting for transfers between devices  233 us (40%)
  matrix products  50.8 us (9%)
  starting transfers between devices  23.9 us (4%)
  local copies, waits for them, and re-layouts  12.4 us (2%)
    all_to_all x2, blocking collectives, section_layer(): lax.all_to_all(outgoing, 'expert', split_axis=0, concat_axis=0, tiled=True)  250 us
    all_to_all x2, waiting for transfers between devices, section_layer(): lax.all_to_all(jnp.einsum('ncf,fd->ncd', hidden, down_w, preferred_elemen...  204 us
    ppermute x2, waiting for transfers between devices, shifted(): return lax.ppermute(block, axis, route)  28.9 us
    all_to_all x2, starting transfers between devices, section_layer(): lax.all_to_all(jnp.einsum('ncf,fd->ncd', hidden, down_w, preferred_elemen...  23.8 us
    dot_general x2, matrix products, section_layer(): jnp.einsum('ncf,fd->ncd', hidden, down_w, preferred_element_type=jnp.floa...  23.2 us
  transfers between devices with their start and end apart: 4, of which 4 were waited for; matrix products, arithmetic and copies ran while one was open for 2% of the time, Pallas kernels for 0%

commit v1 on v0

v1 whole, which is shorter than its diff:
```python
import jax
import jax.numpy as jnp
from jax import lax
from jax.sharding import PartitionSpec as P

D = 4096
SLOTS = 40
NX = 4
NZ = 4
CHUNKS = (((0,), 0, 40), ((2,), 0, 40), ((1, 3), 0, 24), ((1, 3), 24, 16))


def expert_at(z, x):
    return (z % NZ) * NX + (x % NX)


def along_x(block, flip):
    route = [(expert_at(z, x), expert_at(z, x ^ flip)) for z in range(NZ) for x in range(NX)]
    return lax.ppermute(block, "expert", route)


def along_z(block, distance):
    route = [(expert_at(z, x), expert_at(z + distance, x)) for z in range(NZ) for x in range(NX)]
    return lax.ppermute(block, "expert", route)


def to_next(block, distance):
    sections = lax.axis_size("section")
    if distance == 0:
        return lax.ppermute(block, "section", [(s, (s + 1) % sections) for s in range(sections)])
    route = [
        (s * NZ * NX + expert_at(z, x), (s + 1) % sections * NZ * NX + expert_at(z + distance, x))
        for s in range(sections)
        for z in range(NZ)
        for x in range(NX)
    ]
    return lax.ppermute(block, ("section", "expert"), route)


def rms_norm(values, gain):
    wide = values.astype(jnp.float32)
    meansq = jnp.mean(wide * wide, axis=-1, keepdims=True)
    return (wide * lax.rsqrt(meansq + 1e-06) * gain).astype(jnp.bfloat16)


def blocks_of():
    return [(k, first, count) for ks, first, count in CHUNKS for k in ks]


def tables(ids, weights):
    rows = ids.shape[0]
    z = lax.axis_index("expert") // NX
    pair = lax.axis_index("expert") % NX // 2
    experts = jnp.arange(2 * NZ, dtype=jnp.int32)
    hit_k = ids[:, :, None] == experts
    hit = jnp.any(hit_k, axis=1)
    share = jnp.sum(jnp.where(hit_k, weights.astype(jnp.float32)[:, :, None], 0.0), axis=1)
    before = jnp.tril(jnp.ones((rows, rows), jnp.bfloat16), -1)
    ranks = jnp.dot(before, hit.astype(jnp.bfloat16), preferred_element_type=jnp.float32)
    code = jnp.where(hit, ranks, -1.0)
    places, slots = [], []
    for k, first, count in blocks_of():
        for other in range(2):
            places += [(k, other)] * count
            slots += list(range(first, first + count))
    ks = jnp.array([p[0] for p in places], jnp.int32)
    others = jnp.array([p[1] for p in places], jnp.int32)
    named = 2 * ((z + ks) % NZ) + (pair ^ others)
    hot = (named[:, None] == experts).astype(jnp.bfloat16)
    code_at = lax.dot_general(hot, code.astype(jnp.bfloat16), (((1,), (1,)), ((), ())), preferred_element_type=jnp.float32)
    share_at = lax.dot_general(hot, share.astype(jnp.bfloat16), (((1,), (1,)), ((), ())), preferred_element_type=jnp.float32)
    match = code_at == jnp.array(slots, jnp.float32)[:, None]
    select = match.astype(jnp.bfloat16)
    combine = jnp.where(match, share_at, 0.0).astype(jnp.bfloat16)
    return select, combine


def fence(*values):
    return lax.optimization_barrier(values)


def hidden_rows(rows, weights):
    gate = jnp.dot(rows, weights[0], preferred_element_type=jnp.float32)
    up = jnp.dot(rows, weights[1], preferred_element_type=jnp.float32)
    return (jax.nn.silu(gate) * up).astype(jnp.bfloat16)


def down_rows(hidden, got, both_down):
    both = jnp.concatenate([hidden, got], axis=1)
    out = jnp.dot(both, both_down, preferred_element_type=jnp.float32).astype(jnp.bfloat16)
    return jnp.split(out, 2, axis=0)


def gather_pair(blocks):
    count = blocks[0].shape[0] // 2
    own = [b[:count] for b in blocks]
    other = [b[count:] for b in blocks]
    if len(blocks) == 1:
        return own[0], other[0]
    return jnp.concatenate(own, axis=0), jnp.concatenate(other, axis=0)


def across(blocks):
    own, other = gather_pair(blocks)
    return jnp.concatenate([own, along_x(other, 3)], axis=0)


def section_layer(state, gain, weights, both_down, ids, shares, first):
    select, combine = tables(ids, shares)
    normed = rms_norm(state, gain)
    picked = jnp.dot(select, normed, preferred_element_type=jnp.float32).astype(jnp.bfloat16)
    parts = []
    at = 0
    for _, _, count in blocks_of():
        parts.append(picked[at : at + 2 * count])
        at += 2 * count
    p_own, p_two, p_a1, p_a3, p_b1, p_b3 = parts

    two = along_z(p_two, 2)
    rows_own = across([p_own])
    near_own = rows_own if first else along_x(rows_own, 1)
    two, rows_own, near_own, combine, state, p_a1, p_a3 = fence(two, rows_own, near_own, combine, state, p_a1, p_a3)
    a1 = along_z(p_a1, 1)
    a3 = along_z(p_a3, -1)
    rows_two = across([two])
    combine = to_next(combine, 0)
    a1, a3, rows_two, combine, p_b1, p_b3 = fence(a1, a3, rows_two, combine, p_b1, p_b3)
    b1 = along_z(p_b1, 1)
    b3 = along_z(p_b3, -1)
    near_two = along_x(rows_two, 1)
    rows_a = across([a1, a3])
    b1, b3, near_two, rows_two, rows_a, near_own, state, both_down = fence(
        b1, b3, near_two, rows_two, rows_a, near_own, state, both_down
    )
    near_a = along_x(rows_a, 1)
    next_state = to_next(state, 0)
    got_two = along_x(hidden_rows(near_two, weights), 1)
    rows_b = across([b1, b3])
    done_two, far_two = down_rows(hidden_rows(rows_two, weights), got_two, both_down)
    done_two, far_two, rows_b = fence(done_two, far_two, rows_b)
    r_two = to_next(done_two, -2)
    far_two = along_x(far_two, 3)
    near_a, rows_a, rows_b, rows_own, near_own, r_two, far_two = fence(
        near_a, rows_a, rows_b, rows_own, near_own, r_two, far_two
    )
    f_two = to_next(far_two, -2)
    near_b = along_x(rows_b, 1)
    got_a = along_x(hidden_rows(near_a, weights), 1)
    near_own = along_x(rows_own, 1) if first else near_own
    hid_a = hidden_rows(rows_a, weights)
    f_two, near_b, rows_b, got_a, hid_a, near_own, rows_own, next_state = fence(
        f_two, near_b, rows_b, got_a, hid_a, near_own, rows_own, next_state
    )
    done_a, far_a = down_rows(hid_a, got_a, both_down)
    got_b = along_x(hidden_rows(near_b, weights), 1)
    got_own = along_x(hidden_rows(near_own, weights), 1)
    half = done_a.shape[0] // 2
    r_a1 = to_next(done_a[:half], -1)
    r_a3 = to_next(done_a[half:], 1)
    far_a = along_x(far_a, 3)
    hid_b = hidden_rows(rows_b, weights)
    hid_own = hidden_rows(rows_own, weights)
    r_a1, r_a3, far_a, got_b, got_own, hid_b, hid_own = fence(r_a1, r_a3, far_a, got_b, got_own, hid_b, hid_own)
    f_a1 = to_next(far_a[:half], -1)
    f_a3 = to_next(far_a[half:], 1)
    done_b, far_b = down_rows(hid_b, got_b, both_down)
    far_b = along_x(far_b, 3)
    done_own, far_own = down_rows(hid_own, got_own, both_down)
    r_own = to_next(done_own, 0)
    far_own = along_x(far_own, 3)
    f_a1, f_a3, done_b, far_b, r_own, far_own = fence(f_a1, f_a3, done_b, far_b, r_own, far_own)
    half = done_b.shape[0] // 2
    r_b1 = to_next(done_b[:half], -1)
    r_b3 = to_next(done_b[half:], 1)
    f_b1 = to_next(far_b[:half], -1)
    f_b3 = to_next(far_b[half:], 1)
    f_own = to_next(far_own, 0)
    merged = jnp.concatenate(
        [r_own, f_own, r_two, f_two, r_a1, f_a1, r_a3, f_a3, r_b1, f_b1, r_b3, f_b3], axis=0
    )
    mixed = lax.dot_general(combine, merged, (((0,), (0,)), ((), ())), preferred_element_type=jnp.float32)
    return (next_state.astype(jnp.float32) + mixed).astype(jnp.bfloat16)


def per_device(tokens, norm_gain, w_gate, w_up, w_down, route_ids, route_weights):
    state = tokens
    weights = (w_gate[0], w_up[0])
    both_down = jnp.concatenate([w_down[0], along_x(w_down[0], 1)], axis=0)
    for t in range(route_ids.shape[0]):
        state = section_layer(state, norm_gain[0], weights, both_down, route_ids[t], route_weights[t], t == 0)
    return state


def solution(mesh):
    in_specs = (
        P(("section", "expert"), None),
        P("section", None),
        P("section", None, "expert"),
        P("section", None, "expert"),
        P("section", "expert", None),
        P(None, ("section", "expert"), None),
        P(None, ("section", "expert"), None),
    )
    out_specs = P(("section", "expert"), None)
    return jax.shard_map(
        per_device, mesh=mesh, in_specs=in_specs, out_specs=out_specs, check_vma=False
    )
```

time: 583 us -> 436 us (0.75)
  blocking collectives: 250 us -> 0 us
  starting transfers between devices: 23.9 us -> 107 us
  waiting for transfers between devices: 233 us -> 261 us
  matrix products: 50.8 us -> 37.5 us
    all_to_all x2 -> x0, blocking collectives: 250 us -> none  [section_layer(): lax.all_to_all(outgoing, 'expert', split_axis=0, concat_axis=0, tiled=True)]
    ppermute x2 -> x71, waiting for transfers between devices: 28.9 us -> 261 us  [the longest x20 117 us: to_next(): return lax.ppermute(block, ('section', 'expert'), route)]
    all_to_all x2 -> x0, waiting for transfers between devices: 204 us -> none  [section_layer(): lax.all_to_all(jnp.einsum('ncf,fd->ncd', hidden, down_w, preferred_elemen...]
    ppermute x2 -> x71, starting transfers between devices: 0.09 us -> 107 us  [the longest x33 45.7 us: along_x(): return lax.ppermute(block, 'expert', route)]
    all_to_all x2 -> x0, starting transfers between devices: 23.8 us -> none  [section_layer(): lax.all_to_all(jnp.einsum('ncf,fd->ncd', hidden, down_w, preferred_elemen...]
    dot_general x12 -> x48, matrix products: 50.8 us -> 37.5 us  [the longest x16 10 us: hidden_rows(): gate = jnp.dot(rows, weights[0], preferred_element_type=jnp.float32)]
  transfers between devices with their start and end apart: 4 -> 71, of which waited for: 4 -> 42; matrix products, arithmetic and copies ran while one was open for 2% -> 7% of each run, Pallas kernels for 0% -> 0%
where the time goes in v1:
time: 436 us; the launch traced here: 428 us
  waiting for transfers between devices  261 us (60%)
  starting transfers between devices  107 us (25%)
  matrix products  37.5 us (9%)
  local copies, waits for them, and re-layouts  14.7 us (3%)
  other arithmetic  6.48 us (1%)
    ppermute x20, waiting for transfers between devices, to_next(): return lax.ppermute(block, ('section', 'expert'), route)  117 us
    ppermute x10, waiting for transfers between devices, along_z(): return lax.ppermute(block, 'expert', route)  55.1 us
    ppermute x33, waiting for transfers between devices, along_x(): return lax.ppermute(block, 'expert', route)  49.4 us
    ppermute x33, starting transfers between devices, along_x(): return lax.ppermute(block, 'expert', route)  45.7 us
    ppermute x8, waiting for transfers between devices, to_next(): lax.ppermute(block, 'section', [(s, (s + 1) % sections) for s in range(se...  39.6 us
    ppermute x10, starting transfers between devices, along_z(): return lax.ppermute(block, 'expert', route)  27.5 us
    ppermute x20, starting transfers between devices, to_next(): return lax.ppermute(block, ('section', 'expert'), route)  24.3 us
    dot_general x16, matrix products, hidden_rows(): gate = jnp.dot(rows, weights[0], preferred_element_type=jnp.float32)  10 us
  transfers between devices with their start and end apart: 71, of which 42 were waited for; matrix products, arithmetic and copies ran while one was open for 7% of the time, Pallas kernels for 0%

profile of v1, /device:TPU:32, one launch (start us, length us, event | category | flops | bytes accessed | tf_op | source)
XLA Modules:
  0.0 428.2 jit_solution(13940666874458917212)
XLA Ops:
  9.6 6.4 %collective-permute-start = (bf16[80,4096]{1,0:T(8,128)(2,1)S(1)}, bf16[80,4096]{1,0:T(8,128)(2,1)S(1)}, u32[]{:S(2)}, u32[]{:S(2)}) collective-permute-start(bf16[80,4096]{1,0:T(8,128)(2,1)S(1)} %slice.226), channel_id=1, source_target_pairs={{0,8},{1,9},{2,10},{3,11},{4,12},{5,13},{6,14},{7,15},{8,0},{9,1},... | collective-permute-start | bytes 1966088 | tf_op jit(solution)/shard_map/ppermute | solution.py:24
  17.5 27.1 %collective-permute-done = bf16[80,4096]{1,0:T(8,128)(2,1)S(1)} collective-permute-done((bf16[80,4096]{1,0:T(8,128)(2,1)S(1)}, bf16[80,4096]{1,0:T(8,128)(2,1)S(1)}, u32[]{:S(2)}, u32[]{:S(2)}) %collective-permute-start) | collective-permute-done | bytes 655392 | tf_op jit(solution)/shard_map/ppermute | solution.py:24
  54.4 13.7 %collective-permute-done.5 = bf16[320,128]{1,0:T(8,128)(2,1)S(1)} collective-permute-done((bf16[320,128]{1,0:T(8,128)(2,1)S(1)}, bf16[320,128]{1,0:T(8,128)(2,1)S(1)}, u32[]{:S(2)}, u32[]{:S(2)}) %collective-permute-start.5) | collective-permute-done | bytes 81952 | tf_op jit(solution)/shard_map/ppermute | solution.py:30
  75.2 4.3 %collective-permute-done.9 = bf16[48,4096]{1,0:T(8,128)(2,1)S(1)} collective-permute-done((bf16[48,4096]{1,0:T(8,128)(2,1)S(1)}, bf16[48,4096]{1,0:T(8,128)(2,1)S(1)}, u32[]{:S(2)}, u32[]{:S(2)}) %collective-permute-start.9) | collective-permute-done | bytes 393248 | tf_op jit(solution)/shard_map/ppermute | solution.py:19
  79.6 7.5 %collective-permute-done.10 = bf16[384,4096]{1,0:T(8,128)(2,1)} collective-permute-done((bf16[384,4096]{1,0:T(8,128)(2,1)S(1)}, bf16[384,4096]{1,0:T(8,128)(2,1)}, u32[]{:S(2)}, u32[]{:S(2)}) %collective-permute-start.10) | collective-permute-done | bytes 3145760 | tf_op jit(solution)/shard_map/ppermute | solution.py:19
  90.8 8.5 %collective-permute-done.8 = bf16[80,4096]{1,0:T(8,128)(2,1)S(1)} collective-permute-done((bf16[80,4096]{1,0:T(8,128)(2,1)S(1)}, bf16[80,4096]{1,0:T(8,128)(2,1)S(1)}, u32[]{:S(2)}, u32[]{:S(2)}) %collective-permute-start.8) | collective-permute-done | bytes 655392 | tf_op jit(solution)/shard_map/ppermute | solution.py:19
  113.8 13.8 %collective-permute-done.14 = bf16[40,4096]{1,0:T(8,128)(2,1)S(1)} collective-permute-done((bf16[40,4096]{1,0:T(8,128)(2,1)S(1)}, bf16[40,4096]{1,0:T(8,128)(2,1)S(1)}, u32[]{:S(2)}, u32[]{:S(2)}) %collective-permute-start.14) | collective-permute-done | bytes 327712 | tf_op jit(solution)/shard_map/ppermute | solution.py:37
  138.7 13.7 %collective-permute-done.16 = bf16[40,4096]{1,0:T(8,128)(2,1)S(1)} collective-permute-done((bf16[40,4096]{1,0:T(8,128)(2,1)S(1)}, bf16[40,4096]{1,0:T(8,128)(2,1)S(1)}, u32[]{:S(2)}, u32[]{:S(2)}) %collective-permute-start.16) | collective-permute-done | bytes 327712 | tf_op jit(solution)/shard_map/ppermute | solution.py:37
  170.8 8.9 %collective-permute-done.21 = bf16[24,4096]{1,0:T(8,128)(2,1)S(1)} collective-permute-done((bf16[24,4096]{1,0:T(8,128)(2,1)S(1)}, bf16[24,4096]{1,0:T(8,128)(2,1)S(1)}, u32[]{:S(2)}, u32[]{:S(2)}) %collective-permute-start.21) | collective-permute-done | bytes 196640 | tf_op jit(solution)/shard_map/ppermute | solution.py:37
  193.4 5.6 %collective-permute-done.26 = bf16[24,4096]{1,0:T(8,128)(2,1)} collective-permute-done((bf16[24,4096]{1,0:T(8,128)(2,1)}, bf16[24,4096]{1,0:T(8,128)(2,1)}, u32[]{:S(2)}, u32[]{:S(2)}) %collective-permute-start.26) | collective-permute-done | bytes 196640 | tf_op jit(solution)/shard_map/ppermute | solution.py:37
  199.0 8.7 %collective-permute-done.27 = bf16[24,4096]{1,0:T(8,128)(2,1)} collective-permute-done((bf16[24,4096]{1,0:T(8,128)(2,1)}, bf16[24,4096]{1,0:T(8,128)(2,1)}, u32[]{:S(2)}, u32[]{:S(2)}) %collective-permute-start.27) | collective-permute-done | bytes 196640 | tf_op jit(solution)/shard_map/ppermute | solution.py:37
  228.6 4.8 %collective-permute-start.37 = (bf16[40,4096]{1,0:T(8,128)(2,1)S(1)}, bf16[40,4096]{1,0:T(8,128)(2,1)S(1)}, u32[]{:S(2)}, u32[]{:S(2)}) collective-permute-start(bf16[40,4096]{1,0:T(8,128)(2,1)S(1)} %get-tuple-element.214), channel_id=1, source_target_pairs={{0,3},{1,2},{2,1},{3,0},{4,7},{5,6},{6,5},{7,4},{8,11},{9,10},{10,... | collective-permute-start | bytes 983048 | tf_op jit(solution)/shard_map/ppermute | solution.py:19
  233.8 4.3 %collective-permute-start.36 = (bf16[80,4096]{1,0:T(8,128)(2,1)S(1)}, bf16[80,4096]{1,0:T(8,128)(2,1)S(1)}, u32[]{:S(2)}, u32[]{:S(2)}) collective-permute-start(bf16[80,4096]{1,0:T(8,128)(2,1)S(1)} %slice.235), channel_id=1, source_target_pairs={{0,8},{1,9},{2,10},{3,11},{4,12},{5,13},{6,14},{7,15},{8,0},{9,1},... | collective-permute-start | bytes 1966088 | tf_op jit(solution)/shard_map/ppermute | solution.py:24
  240.1 24.5 %collective-permute-done.36 = bf16[80,4096]{1,0:T(8,128)(2,1)S(1)} collective-permute-done((bf16[80,4096]{1,0:T(8,128)(2,1)S(1)}, bf16[80,4096]{1,0:T(8,128)(2,1)S(1)}, u32[]{:S(2)}, u32[]{:S(2)}) %collective-permute-start.36) | collective-permute-done | bytes 655392 | tf_op jit(solution)/shard_map/ppermute | solution.py:24
  275.2 11.9 %collective-permute-done.42 = bf16[320,128]{1,0:T(8,128)(2,1)S(1)} collective-permute-done((bf16[320,128]{1,0:T(8,128)(2,1)S(1)}, bf16[320,128]{1,0:T(8,128)(2,1)S(1)}, u32[]{:S(2)}, u32[]{:S(2)}) %collective-permute-start.42) | collective-permute-done | bytes 81952 | tf_op jit(solution)/shard_map/ppermute | solution.py:30
  293.4 6.6 %collective-permute-done.46 = bf16[48,4096]{1,0:T(8,128)(2,1)S(1)} collective-permute-done((bf16[48,4096]{1,0:T(8,128)(2,1)S(1)}, bf16[48,4096]{1,0:T(8,128)(2,1)S(1)}, u32[]{:S(2)}, u32[]{:S(2)}) %collective-permute-start.46) | collective-permute-done | bytes 393248 | tf_op jit(solution)/shard_map/ppermute | solution.py:19
  322.4 12.0 %collective-permute-done.50 = bf16[40,4096]{1,0:T(8,128)(2,1)S(1)} collective-permute-done((bf16[40,4096]{1,0:T(8,128)(2,1)S(1)}, bf16[40,4096]{1,0:T(8,128)(2,1)S(1)}, u32[]{:S(2)}, u32[]{:S(2)}) %collective-permute-start.50) | collective-permute-done | bytes 327712 | tf_op jit(solution)/shard_map/ppermute | solution.py:37
  342.2 17.5 %collective-permute-done.52 = bf16[40,4096]{1,0:T(8,128)(2,1)S(1)} collective-permute-done((bf16[40,4096]{1,0:T(8,128)(2,1)S(1)}, bf16[40,4096]{1,0:T(8,128)(2,1)S(1)}, u32[]{:S(2)}, u32[]{:S(2)}) %collective-permute-start.52) | collective-permute-done | bytes 327712 | tf_op jit(solution)/shard_map/ppermute | solution.py:37
  369.7 5.6 %collective-permute-done.56 = bf16[24,4096]{1,0:T(8,128)(2,1)S(1)} collective-permute-done((bf16[24,4096]{1,0:T(8,128)(2,1)S(1)}, bf16[24,4096]{1,0:T(8,128)(2,1)S(1)}, u32[]{:S(2)}, u32[]{:S(2)}) %collective-permute-start.56) | collective-permute-done | bytes 196640 | tf_op jit(solution)/shard_map/ppermute | solution.py:37
  375.3 4.4 %collective-permute-done.57 = bf16[24,4096]{1,0:T(8,128)(2,1)S(1)} collective-permute-done((bf16[24,4096]{1,0:T(8,128)(2,1)S(1)}, bf16[24,4096]{1,0:T(8,128)(2,1)S(1)}, u32[]{:S(2)}, u32[]{:S(2)}) %collective-permute-start.57) | collective-permute-done | bytes 196640 | tf_op jit(solution)/shard_map/ppermute | solution.py:37
  380.9 4.5 %collective-permute-start.64 = (bf16[40,4096]{1,0:T(8,128)(2,1)S(1)}, bf16[40,4096]{1,0:T(8,128)(2,1)S(1)}, u32[]{:S(2)}, u32[]{:S(2)}) collective-permute-start(bf16[40,4096]{1,0:T(8,128)(2,1)S(1)} %get-tuple-element.226), channel_id=1, source_target_pairs={{0,16},{16,32},{32,48},{48,64},{64,80},{80,96},{96,112},{112,128},... | collective-permute-start | bytes 983048 | tf_op jit(solution)/shard_map/ppermute | solution.py:30
  393.8 7.4 %collective-permute-done.61 = bf16[24,4096]{1,0:T(8,128)(2,1)S(1)} collective-permute-done((bf16[24,4096]{1,0:T(8,128)(2,1)S(1)}, bf16[24,4096]{1,0:T(8,128)(2,1)S(1)}, u32[]{:S(2)}, u32[]{:S(2)}) %collective-permute-start.61) | collective-permute-done | bytes 196640 | tf_op jit(solution)/shard_map/ppermute | solution.py:37
  401.2 4.4 %collective-permute-done.62 = bf16[24,4096]{1,0:T(8,128)(2,1)S(1)} collective-permute-done((bf16[24,4096]{1,0:T(8,128)(2,1)S(1)}, bf16[24,4096]{1,0:T(8,128)(2,1)S(1)}, u32[]{:S(2)}, u32[]{:S(2)}) %collective-permute-start.62) | collective-permute-done | bytes 196640 | tf_op jit(solution)/shard_map/ppermute | solution.py:37
  409.3 6.9 %collective-permute-done.66 = bf16[40,4096]{1,0:T(8,128)(2,1)S(1)} collective-permute-done((bf16[40,4096]{1,0:T(8,128)(2,1)S(1)}, bf16[40,4096]{1,0:T(8,128)(2,1)S(1)}, u32[]{:S(2)}, u32[]{:S(2)}) %collective-permute-start.66) | collective-permute-done | bytes 327712 | tf_op jit(solution)/shard_map/ppermute | solution.py:30
  (288 shorter events, 193.4 us)
Async XLA Ops:
  9.6 35.0 %collective-permute-start = (bf16[80,4096]{1,0:T(8,128)(2,1)S(1)}, bf16[80,4096]{1,0:T(8,128)(2,1)S(1)}, u32[]{:S(2)}, u32[]{:S(2)}) collective-permute-start(bf16[80,4096]{1,0:T(8,128)(2,1)S(1)} %slice.226), channel_id=1, source_target_pairs={{0,8},{1,9},{2,10},{3,11},{4,12},{5,13},{6,14},{7,15},{8,0},{9,1},... | collective-permute-start | bytes 1966088 | tf_op jit(solution)/shard_map/ppermute | solution.py:24
  15.9 71.1 %collective-permute-start.10 = (bf16[384,4096]{1,0:T(8,128)(2,1)S(1)}, bf16[384,4096]{1,0:T(8,128)(2,1)}, u32[]{:S(2)}, u32[]{:S(2)}) collective-permute-start(bf16[384,4096]{1,0:T(8,128)(2,1)S(1)} %bitcast.163), channel_id=1, source_target_pairs={{0,1},{1,0},{2,3},{3,2},{4,5},{5,4},{6,7},{7,6},{8,9},{9,8},{10,11... | collective-permute-start | bytes 9437192 | tf_op jit(solution)/shard_map/ppermute | solution.py:19
  46.0 22.2 %collective-permute-start.2 = (bf16[48,4096]{1,0:T(8,128)(2,1)S(1)}, bf16[48,4096]{1,0:T(8,128)(2,1)S(1)}, u32[]{:S(2)}, u32[]{:S(2)}) collective-permute-start(bf16[48,4096]{1,0:T(8,128)(2,1)S(1)} %get-tuple-element.106), channel_id=1, source_target_pairs={{0,4},{1,5},{2,6},{3,7},{4,8},{5,9},{6,10},{7,11},{8,12},{9,13},{1... | collective-permute-start | bytes 1179656 | tf_op jit(solution)/shard_map/ppermute | solution.py:24
  46.0 22.2 %collective-permute-start.3 = (bf16[48,4096]{1,0:T(8,128)(2,1)S(1)}, bf16[48,4096]{1,0:T(8,128)(2,1)S(1)}, u32[]{:S(2)}, u32[]{:S(2)}) collective-permute-start(bf16[48,4096]{1,0:T(8,128)(2,1)S(1)} %get-tuple-element.107), channel_id=1, source_target_pairs={{0,12},{1,13},{2,14},{3,15},{4,0},{5,1},{6,2},{7,3},{8,4},{9,5},{1... | collective-permute-start | bytes 1179656 | tf_op jit(solution)/shard_map/ppermute | solution.py:24
  71.1 28.2 %collective-permute-start.8 = (bf16[80,4096]{1,0:T(8,128)(2,1)S(1)}, bf16[80,4096]{1,0:T(8,128)(2,1)S(1)}, u32[]{:S(2)}, u32[]{:S(2)}) collective-permute-start(bf16[80,4096]{1,0:T(8,128)(2,1)S(1)} %pad_maximum_fusion.4), channel_id=1, source_target_pairs={{0,1},{1,0},{2,3},{3,2},{4,5},{5,4},{6,7},{7,6},{8,9},{9,8},{10,11... | collective-permute-start | bytes 1966088 | tf_op jit(solution)/shard_map/ppermute | solution.py:19
  71.1 19.7 %collective-permute-start.6 = (bf16[32,4096]{1,0:T(8,128)(2,1)}, bf16[32,4096]{1,0:T(8,128)(2,1)S(1)}, u32[]{:S(2)}, u32[]{:S(2)}) collective-permute-start(bf16[32,4096]{1,0:T(8,128)(2,1)} %get-tuple-element.110), channel_id=1, source_target_pairs={{0,4},{1,5},{2,6},{3,7},{4,8},{5,9},{6,10},{7,11},{8,12},{9,13},{1... | collective-permute-start | bytes 786440 | tf_op jit(solution)/shard_map/ppermute | solution.py:24
  104.3 24.1 %collective-permute-start.11 = (bf16[96,4096]{1,0:T(8,128)(2,1)S(1)}, bf16[96,4096]{1,0:T(8,128)(2,1)S(1)}, u32[]{:S(2)}, u32[]{:S(2)}) collective-permute-start(bf16[96,4096]{1,0:T(8,128)(2,1)S(1)} %pad_maximum_fusion.1), channel_id=1, source_target_pairs={{0,1},{1,0},{2,3},{3,2},{4,5},{5,4},{6,7},{7,6},{8,9},{9,8},{10,11... | collective-permute-start | bytes 2359304 | tf_op jit(solution)/shard_map/ppermute | solution.py:19
  112.6 26.1 %collective-permute-start.20 = (bf16[128,4096]{1,0:T(8,128)(2,1)S(1)}, bf16[128,4096]{1,0:T(8,128)(2,1)S(1)}, u32[]{:S(2)}, u32[]{:S(2)}) collective-permute-start(bf16[128,4096]{1,0:T(8,128)(2,1)S(1)} %copy-done.4), channel_id=1, source_target_pairs={{0,16},{16,32},{32,48},{48,64},{64,80},{80,96},{96,112},{112,128},... | collective-permute-start | bytes 3145736 | tf_op jit(solution)/shard_map/ppermute | solution.py:30
  129.8 26.8 %collective-permute-start.19 = (bf16[80,4096]{1,0:T(8,128)(2,1)S(1)}, bf16[80,4096]{1,0:T(8,128)(2,1)S(1)}, u32[]{:S(2)}, u32[]{:S(2)}) collective-permute-start(bf16[80,4096]{1,0:T(8,128)(2,1)S(1)} %pad_maximum_fusion.3), channel_id=1, source_target_pairs={{0,1},{1,0},{2,3},{3,2},{4,5},{5,4},{6,7},{7,6},{8,9},{9,8},{10,11... | collective-permute-start | bytes 1966088 | tf_op jit(solution)/shard_map/ppermute | solution.py:19
  131.8 24.8 %collective-permute-start.17 = (bf16[64,4096]{1,0:T(8,128)(2,1)S(1)}, bf16[64,4096]{1,0:T(8,128)(2,1)S(1)}, u32[]{:S(2)}, u32[]{:S(2)}) collective-permute-start(bf16[64,4096]{1,0:T(8,128)(2,1)S(1)} %pad_maximum_fusion.7), channel_id=1, source_target_pairs={{0,1},{1,0},{2,3},{3,2},{4,5},{5,4},{6,7},{7,6},{8,9},{9,8},{10,11... | collective-permute-start | bytes 1572872 | tf_op jit(solution)/shard_map/ppermute | solution.py:19
  131.9 20.5 %collective-permute-start.16 = (bf16[40,4096]{1,0:T(8,128)(2,1)S(1)}, bf16[40,4096]{1,0:T(8,128)(2,1)S(1)}, u32[]{:S(2)}, u32[]{:S(2)}) collective-permute-start(bf16[40,4096]{1,0:T(8,128)(2,1)S(1)} %collective-permute-done.15), channel_id=1, source_target_pairs={{0,24},{1,25},{2,26},{3,27},{4,28},{5,29},{6,30},{7,31},{8,16},{9,... | collective-permute-start | bytes 983048 | tf_op jit(solution)/shard_map/ppermute | solution.py:37
  183.3 24.4 %collective-permute-start.29 = (bf16[40,4096]{1,0:T(8,128)(2,1)}, bf16[40,4096]{1,0:T(8,128)(2,1)}, u32[]{:S(2)}, u32[]{:S(2)}) collective-permute-start(bf16[40,4096]{1,0:T(8,128)(2,1)} %get-tuple-element.232), channel_id=1, source_target_pairs={{0,16},{16,32},{32,48},{48,64},{64,80},{80,96},{96,112},{112,128},... | collective-permute-start | bytes 983048 | tf_op jit(solution)/shard_map/ppermute | solution.py:30
  183.3 24.4 %collective-permute-start.30 = (bf16[40,4096]{1,0:T(8,128)(2,1)}, bf16[40,4096]{1,0:T(8,128)(2,1)}, u32[]{:S(2)}, u32[]{:S(2)}) collective-permute-start(bf16[40,4096]{1,0:T(8,128)(2,1)} %get-tuple-element.231), channel_id=1, source_target_pairs={{0,3},{1,2},{2,1},{3,0},{4,7},{5,6},{6,5},{7,4},{8,11},{9,10},{10,... | collective-permute-start | bytes 983048 | tf_op jit(solution)/shard_map/ppermute | solution.py:19
  188.4 19.3 %collective-permute-start.28 = (bf16[32,4096]{1,0:T(8,128)(2,1)}, bf16[32,4096]{1,0:T(8,128)(2,1)}, u32[]{:S(2)}, u32[]{:S(2)}) collective-permute-start(bf16[32,4096]{1,0:T(8,128)(2,1)} %get-tuple-element.239), channel_id=1, source_target_pairs={{0,3},{1,2},{2,1},{3,0},{4,7},{5,6},{6,5},{7,4},{8,11},{9,10},{10,... | collective-permute-start | bytes 786440 | tf_op jit(solution)/shard_map/ppermute | solution.py:19
  233.8 30.9 %collective-permute-start.36 = (bf16[80,4096]{1,0:T(8,128)(2,1)S(1)}, bf16[80,4096]{1,0:T(8,128)(2,1)S(1)}, u32[]{:S(2)}, u32[]{:S(2)}) collective-permute-start(bf16[80,4096]{1,0:T(8,128)(2,1)S(1)} %slice.235), channel_id=1, source_target_pairs={{0,8},{1,9},{2,10},{3,11},{4,12},{5,13},{6,14},{7,15},{8,0},{9,1},... | collective-permute-start | bytes 1966088 | tf_op jit(solution)/shard_map/ppermute | solution.py:24
  240.0 24.7 %collective-permute-start.38 = (bf16[80,4096]{1,0:T(8,128)(2,1)S(1)}, bf16[80,4096]{1,0:T(8,128)(2,1)S(1)}, u32[]{:S(2)}, u32[]{:S(2)}) collective-permute-start(bf16[80,4096]{1,0:T(8,128)(2,1)S(1)} %pad_maximum_fusion.5), channel_id=1, source_target_pairs={{0,1},{1,0},{2,3},{3,2},{4,5},{5,4},{6,7},{7,6},{8,9},{9,8},{10,11... | collective-permute-start | bytes 1966088 | tf_op jit(solution)/shard_map/ppermute | solution.py:19
  267.2 20.4 %collective-permute-start.39 = (bf16[48,4096]{1,0:T(8,128)(2,1)S(1)}, bf16[48,4096]{1,0:T(8,128)(2,1)S(1)}, u32[]{:S(2)}, u32[]{:S(2)}) collective-permute-start(bf16[48,4096]{1,0:T(8,128)(2,1)S(1)} %get-tuple-element.155), channel_id=1, source_target_pairs={{0,4},{1,5},{2,6},{3,7},{4,8},{5,9},{6,10},{7,11},{8,12},{9,13},{1... | collective-permute-start | bytes 1179656 | tf_op jit(solution)/shard_map/ppermute | solution.py:24
  267.5 20.0 %collective-permute-start.40 = (bf16[48,4096]{1,0:T(8,128)(2,1)S(1)}, bf16[48,4096]{1,0:T(8,128)(2,1)S(1)}, u32[]{:S(2)}, u32[]{:S(2)}) collective-permute-start(bf16[48,4096]{1,0:T(8,128)(2,1)S(1)} %get-tuple-element.156), channel_id=1, source_target_pairs={{0,12},{1,13},{2,14},{3,15},{4,0},{5,1},{6,2},{7,3},{8,4},{9,5},{1... | collective-permute-start | bytes 1179656 | tf_op jit(solution)/shard_map/ppermute | solution.py:24
  311.8 22.6 %collective-permute-start.47 = (bf16[96,4096]{1,0:T(8,128)(2,1)S(1)}, bf16[96,4096]{1,0:T(8,128)(2,1)S(1)}, u32[]{:S(2)}, u32[]{:S(2)}) collective-permute-start(bf16[96,4096]{1,0:T(8,128)(2,1)S(1)} %pad_maximum_fusion.2), channel_id=1, source_target_pairs={{0,1},{1,0},{2,3},{3,2},{4,5},{5,4},{6,7},{7,6},{8,9},{9,8},{10,11... | collective-permute-start | bytes 2359304 | tf_op jit(solution)/shard_map/ppermute | solution.py:19
  318.4 23.8 %collective-permute-start.55 = (bf16[128,4096]{1,0:T(8,128)(2,1)S(1)}, bf16[128,4096]{1,0:T(8,128)(2,1)S(1)}, u32[]{:S(2)}, u32[]{:S(2)}) collective-permute-start(bf16[128,4096]{1,0:T(8,128)(2,1)S(1)} %get-tuple-element.183), channel_id=1, source_target_pairs={{0,16},{16,32},{32,48},{48,64},{64,80},{80,96},{96,112},{112,128},... | collective-permute-start | bytes 3145736 | tf_op jit(solution)/shard_map/ppermute | solution.py:30
  336.1 23.7 %collective-permute-start.53 = (bf16[64,4096]{1,0:T(8,128)(2,1)S(1)}, bf16[64,4096]{1,0:T(8,128)(2,1)S(1)}, u32[]{:S(2)}, u32[]{:S(2)}) collective-permute-start(bf16[64,4096]{1,0:T(8,128)(2,1)S(1)} %pad_maximum_fusion.8), channel_id=1, source_target_pairs={{0,1},{1,0},{2,3},{3,2},{4,5},{5,4},{6,7},{7,6},{8,9},{9,8},{10,11... | collective-permute-start | bytes 1572872 | tf_op jit(solution)/shard_map/ppermute | solution.py:19
  337.9 21.8 %collective-permute-start.52 = (bf16[40,4096]{1,0:T(8,128)(2,1)S(1)}, bf16[40,4096]{1,0:T(8,128)(2,1)S(1)}, u32[]{:S(2)}, u32[]{:S(2)}) collective-permute-start(bf16[40,4096]{1,0:T(8,128)(2,1)S(1)} %collective-permute-done.51), channel_id=1, source_target_pairs={{0,24},{1,25},{2,26},{3,27},{4,28},{5,29},{6,30},{7,31},{8,16},{9,... | collective-permute-start | bytes 983048 | tf_op jit(solution)/shard_map/ppermute | solution.py:37
  380.9 24.6 %collective-permute-start.64 = (bf16[40,4096]{1,0:T(8,128)(2,1)S(1)}, bf16[40,4096]{1,0:T(8,128)(2,1)S(1)}, u32[]{:S(2)}, u32[]{:S(2)}) collective-permute-start(bf16[40,4096]{1,0:T(8,128)(2,1)S(1)} %get-tuple-element.226), channel_id=1, source_target_pairs={{0,16},{16,32},{32,48},{48,64},{64,80},{80,96},{96,112},{112,128},... | collective-permute-start | bytes 983048 | tf_op jit(solution)/shard_map/ppermute | solution.py:30
  385.4 20.2 %collective-permute-start.65 = (bf16[40,4096]{1,0:T(8,128)(2,1)S(1)}, bf16[40,4096]{1,0:T(8,128)(2,1)S(1)}, u32[]{:S(2)}, u32[]{:S(2)}) collective-permute-start(bf16[40,4096]{1,0:T(8,128)(2,1)S(1)} %get-tuple-element.225), channel_id=1, source_target_pairs={{0,3},{1,2},{2,1},{3,0},{4,7},{5,6},{6,5},{7,4},{8,11},{9,10},{10,... | collective-permute-start | bytes 983048 | tf_op jit(solution)/shard_map/ppermute | solution.py:19
  (67 other events, 958.4 us)
